TPU v7x, 32 devices: a whole 2x2x4 slice. The times are simulated.
32 devices in a mesh: grp: 4 (over y, core), sp: 8 (over z, x).
Axes of the slice: x: 2, y: 2, z: 4, core: 2. Of those that a mesh axis runs over, the one named last changes fastest.
Arguments:
- residual: bfloat16 [2048, 4096], P(('grp', 'sp')), may hold values from -6 to 6
- queries: bfloat16 [2048, 4096], P(('grp', 'sp')), may hold values from -60 to 60
- key_value_pairs: bfloat16 [2048, 1024], P(('grp', 'sp')), may hold values from -5 to 5
- out_weight: bfloat16 [4096, 4096], P('sp'), may hold values from -0.09375 to 0.09375
- norm_gain: float32 [4096], replicated, may hold values from 0.5 to 1.5
- amax_history: float32 [4], replicated, may hold values from 2 to 3.5
- doc_ids: int32 [4, 512], P('grp', 'sp'), may hold values from 0 to 5, never falling along the last dimension, each value on 1 to 192 neighbouring positions
- expert_ids: int32 [2048, 8], P(('grp', 'sp')), may hold values from 0 to 15, all different within a row; in each aligned block of 64 rows (0 to 63, 64 to 127, ...) at most 32 rows name the same one
- gate_up_weight: bfloat16 [32, 4096, 768], P(('grp', 'sp')), may hold values from -0.09375 to 0.09375
Outputs:
- after_attention: bfloat16 [2048, 4096], P(('grp', 'sp'))
- expert_hidden: bfloat16 [32, 1024, 384], P(('grp', 'sp'))
- group_amax: float32 [4], P('grp')
Inputs may be any that keep to these rules, and one draw needn't show every extreme that they name: `doc_ids`: within a slice the document number never falls along the tokens. `expert_ids`: the 8 experts of a token are distinct. Among the 64 tokens of one device no expert is named more than 32 times, and on some device some expert is named exactly 32 times.
All inputs are finite; a program needn't handle non-finite values.
Results may differ from a plain program's by a relative error of at most 0.017.
Values may be sent and summed in bfloat16 or wider, within the bound.
A program may use at most 128 MiB of HBM per device.

v0:
```python
import jax
import jax.numpy as jnp
from jax import lax
from jax.sharding import PartitionSpec as P

QUERY_HEAD_SLICE = 32
KEY_VALUE_HEADS = 4
HEAD_SIZE = 128
TOP = 8
HALVES = 2


def activate(rows, unscale, weight):
    width = weight.shape[1] // 2
    gate_up = jnp.dot(rows, weight, preferred_element_type=jnp.float32)
    gate = gate_up[:, :width] * unscale
    upward = gate_up[:, width:] * unscale
    return (jax.nn.silu(gate) * upward).astype(jnp.bfloat16)


def per_device(
    residual,
    queries,
    key_value_pairs,
    out_weight,
    norm_gain,
    amax_history,
    doc_ids,
    expert_ids,
    gate_up_weight,
):
    sequence_parallel_count = lax.axis_size("sp")
    grp_count = lax.axis_size("grp")
    local_row_count = residual.shape[0]
    heads_here = QUERY_HEAD_SLICE // sequence_parallel_count
    query_local = queries.reshape(local_row_count, sequence_parallel_count, heads_here * HEAD_SIZE)
    pair_replicas = jnp.repeat(
        key_value_pairs.reshape(local_row_count, KEY_VALUE_HEADS, 2 * HEAD_SIZE),
        sequence_parallel_count // KEY_VALUE_HEADS,
        axis=1,
    )
    doc_copies = jnp.broadcast_to(
        doc_ids.reshape(local_row_count, 1, 1), (local_row_count, sequence_parallel_count, 1)
    )
    query_heads, pair_head, doc_column = (
        lax.all_to_all(query_local, "sp", split_axis=1, concat_axis=0, tiled=True),
        lax.all_to_all(pair_replicas, "sp", split_axis=1, concat_axis=0, tiled=True),
        lax.all_to_all(doc_copies, "sp", split_axis=1, concat_axis=0, tiled=True),
    )
    slice_length = query_heads.shape[0]
    pair_head = pair_head.reshape(slice_length, 2 * HEAD_SIZE)
    documents = doc_column.reshape(slice_length)
    query_heads = query_heads.reshape(slice_length, heads_here, HEAD_SIZE)
    key_rows = pair_head[:, :HEAD_SIZE]
    value_rows = pair_head[:, HEAD_SIZE:]
    block_rows = min(512, slice_length)
    positions = jnp.arange(slice_length, dtype=jnp.int32)

    def attend(block_index):
        offset = block_index * block_rows
        query_block = lax.dynamic_slice_in_dim(query_heads, offset, block_rows, 0)
        row_positions = offset + jnp.arange(block_rows, dtype=jnp.int32)
        row_documents = lax.dynamic_slice_in_dim(documents, offset, block_rows, 0)
        allowed = (positions[None, :] <= row_positions[:, None]) & (
            documents[None, :] == row_documents[:, None]
        )
        scores = jnp.einsum(
            "bhd,kd->hbk", query_block, key_rows, preferred_element_type=jnp.float32
        ) * HEAD_SIZE ** (-0.5)
        scores = jnp.where(allowed[None], scores, -jnp.inf)
        highest = jnp.max(scores, axis=2, keepdims=True)
        weights = jnp.exp(scores - highest)
        probs = (weights / jnp.sum(weights, axis=2, keepdims=True)).astype(jnp.bfloat16)
        return jnp.einsum(
            "hbk,kd->bhd", probs, value_rows, preferred_element_type=jnp.float32
        ).astype(jnp.bfloat16)

    context = lax.map(attend, jnp.arange(slice_length // block_rows, dtype=jnp.int32))
    block_width = heads_here * HEAD_SIZE
    context = context.reshape(slice_length, block_width)
    projected = lax.psum_scatter(
        jnp.dot(context, out_weight, preferred_element_type=jnp.float32).astype(jnp.bfloat16),
        "sp",
        scatter_dimension=0,
        tiled=True,
    ).astype(jnp.float32)
    after_attention = (residual.astype(jnp.float32) + projected).astype(jnp.bfloat16)
    widened = after_attention.astype(jnp.float32)
    normed = (
        widened * lax.rsqrt(jnp.mean(widened * widened, axis=1, keepdims=True) + 1e-06) * norm_gain
    )
    group_amax = lax.pmax(jnp.max(jnp.abs(normed)).reshape(1), "sp")
    own_history = lax.dynamic_index_in_dim(amax_history, lax.axis_index("grp"), 0, False)
    quantized = jnp.clip(normed * (448.0 / own_history), -448.0, 448.0).astype(jnp.bfloat16)
    experts = grp_count * sequence_parallel_count // HALVES
    most_rows = max(2, local_row_count * TOP // experts)
    routing = expert_ids.reshape(local_row_count * TOP)
    one_hot = (routing[:, None] == jnp.arange(experts, dtype=jnp.int32)[None, :]).astype(jnp.int32)
    rank = jnp.sum((jnp.cumsum(one_hot, axis=0) - one_hot) * one_hot, axis=1)
    slot_index = routing * most_rows + rank
    picker = jnp.arange(experts * most_rows, dtype=jnp.int32)[:, None] == slot_index[None, :]
    picker = jnp.sum(
        picker.reshape(experts * most_rows, local_row_count, TOP).astype(jnp.int32), axis=2
    ).astype(jnp.bfloat16)
    outgoing = jnp.dot(picker, quantized, preferred_element_type=jnp.float32).astype(jnp.bfloat16)
    outgoing = outgoing.reshape(grp_count, experts // grp_count, most_rows, outgoing.shape[1])
    arrived = lax.all_to_all(outgoing, "grp", split_axis=0, concat_axis=0, tiled=True)
    width_model = arrived.shape[3]
    copies = jnp.repeat(arrived, HALVES, axis=1)
    slot_rows = lax.all_to_all(copies, "sp", split_axis=1, concat_axis=1, tiled=True)
    total_rows = grp_count * sequence_parallel_count * most_rows
    flat_rows = slot_rows.reshape(total_rows, width_model)
    unscale = jnp.repeat(amax_history / 448.0, sequence_parallel_count * most_rows)[:, None]
    weight = gate_up_weight[0]
    expert_hidden = activate(flat_rows, unscale, weight)
    return (
        after_attention,
        expert_hidden.reshape(1, total_rows, expert_hidden.shape[1]),
        group_amax,
    )


def solution(mesh):
    in_specs = (
        P(("grp", "sp"), None),
        P(("grp", "sp"), None),
        P(("grp", "sp"), None),
        P("sp", None),
        P(),
        P(),
        P("grp", "sp"),
        P(("grp", "sp"), None),
        P(("grp", "sp"), None, None),
    )
    out_specs = (P(("grp", "sp"), None), P(("grp", "sp"), None, None), P("grp"))
    return jax.shard_map(
        per_device, mesh=mesh, in_specs=in_specs, out_specs=out_specs, check_vma=False
    )
```

profile of v0, /device:TPU:0, one launch (start us, length us, event | category | flops | bytes accessed | tf_op | source)
XLA Modules:
  0.0 421.1 jit_solution(11852679400920719231)
XLA Ops:
  7.2 1.3 broadcast_in_dim.54
  8.4 7.3 %all-to-all-start = ((s32[64,8,1]{0,2,1:T(1,128)}), s32[64,8,1]{0,2,1:T(1,128)S(1)}, u32[]{:S(2)}, u32[]{:S(2)}) async-start(s32[64,8,1]{0,2,1:T(1,128)} %broadcast_in_dim.54), calls=%async_computation | async-start | bytes 8192 | tf_op jit(solution)/shard_map/all_to_all | solution.py:48
  15.7 1.9 copy.85
  17.6 4.5 %all-to-all-done = s32[64,8,1]{0,2,1:T(1,128)S(1)} async-done(((s32[64,8,1]{0,2,1:T(1,128)}), s32[64,8,1]{0,2,1:T(1,128)S(1)}, u32[]{:S(2)}, u32[]{:S(2)}) %all-to-all-start) | async-done | bytes 2080 | tf_op jit(solution)/shard_map/all_to_all | solution.py:48
  22.1 3.5 all-to-all-start.2
  25.6 0.9 copy.86
  26.5 12.3 %all-to-all-done.2 = bf16[64,8,512]{2,0,1:T(8,128)(2,1)S(1)} async-done(((bf16[64,8,512]{2,0,1:T(8,128)(2,1)}), bf16[64,8,512]{2,0,1:T(8,128)(2,1)S(1)}, u32[]{:S(2)}, u32[]{:S(2)}) %all-to-all-start.2) | async-done | bytes 524320 | tf_op jit(solution)/shard_map/all_to_all | solution.py:46
  38.8 0.7 broadcast_in_dim.56
  39.5 3.7 all-to-all-start.1
  43.2 0.0 reduce-scatter.2.cloned.1.call-start
  43.2 0.1 eq.65
  43.3 0.2 fusion.18
  43.5 0.1 reshape.154
  43.7 7.9 %all-to-all-done.1 = bf16[64,8,256]{2,0,1:T(8,128)(2,1)S(1)} async-done(((bf16[64,8,256]{2,0,1:T(8,128)(2,1)}), bf16[64,8,256]{2,0,1:T(8,128)(2,1)S(1)}, u32[]{:S(2)}, u32[]{:S(2)}) %all-to-all-start.1) | async-done | bytes 262176 | tf_op jit(solution)/shard_map/all_to_all | solution.py:47
  51.6 0.7 fusion.21
  52.3 2.1 fusion.37
  54.5 0.8 fusion.10
  55.2 1.4 copy-done.1
  56.6 4.3 %convolution_convert_fusion.1 = bf16[512,4096]{1,0:T(8,128)(2,1)} fusion(bf16[512,512]{0,1:T(8,128)(2,1)S(1)} %bitcast.90, bf16[512,4096]{1,0:T(8,128)(2,1)S(1)} %copy-done.1), kind=kOutput, calls=%fused_computation.4 | convolution fusion | flops 2149580800 | bytes 8912896 | tf_op jit(solution)/shard_map/dot_general | solution.py:82
  60.9 0.0 reduce-scatter.2.cloned.1.call-update
  61.0 0.6 copy-done.4
  61.6 0.1 copy.66
  61.7 0.1 eq.74
  61.8 0.1 eq.70
  61.9 1.2 reduce-window.6
  63.0 0.2 slice_reduce_fusion
  63.3 0.1 fusion.31
  63.4 0.1 reduce_sum.41
  63.5 0.1 copy.69
  63.6 0.1 copy.70
  63.7 0.0 copy-done.5
  63.7 0.6 dynamic_slice.11
  65.0 0.4 convert_reduce_fusion
  65.3 82.7 %reduce-scatter.2.cloned.1.call-done = bf16[64,4096]{1,0:T(8,128)(2,1)} async-done(((bf16[512,4096]{1,0:T(8,128)(2,1)}), bf16[64,4096]{1,0:T(8,128)(2,1)}) %reduce-scatter.2.cloned.1.call-update) | async-done | bytes 524304 | tf_op jit(solution)/shard_map/reduce_scatter | solution.py:81
  148.1 1.3 fusion.11
  149.4 0.0 copy-start
  149.4 1.3 convolution_convert_fusion
  150.8 50.7 %all_to_all.55 = bf16[4,4,32,4096]{3,2,1,0:T(8,128)(2,1)S(1)} all-to-all(bf16[4,4,32,4096]{3,2,1,0:T(8,128)(2,1)S(1)} %bitcast.85), channel_id=1, replica_groups=mesh['grp'=4,'sp'=8] {'grp'}, dimensions={0} | all-to-all | bytes 8388608 | tf_op jit(solution)/shard_map/all_to_all | solution.py:107
  201.5 0.5 copy.71
  202.0 4.3 %broadcast_in_dim.58 = bf16[4,4,2,32,4096]{4,3,0,2,1:T(8,128)(2,1)} broadcast(bf16[4,4,32,4096]{3,2,0,1:T(8,128)(2,1)S(1)} %copy.71), dimensions={0,1,3,4} | broadcast | bytes 12582912 | tf_op jit(solution)/shard_map/broadcast_in_dim | solution.py:109
  206.3 5.0 %all-to-all-start.4 = ((bf16[4,8,32,4096]{3,2,0,1:T(8,128)(2,1)}), bf16[4,8,32,4096]{3,2,0,1:T(8,128)(2,1)}, u32[]{:S(2)}, u32[]{:S(2)}) async-start(bf16[4,8,32,4096]{3,2,0,1:T(8,128)(2,1)} %bitcast.84), calls=%async_computation.5 | async-start | bytes 16777216 | tf_op jit(solution)/shard_map/all_to_all | solution.py:110
  211.2 0.1 broadcast_bitcast_fusion
  211.3 0.8 fusion.17
  212.1 163.2 %pmax.7 = f32[1]{0:T(128)} all-reduce(f32[1]{0:T(128)} %bitcast.23), channel_id=1, replica_groups=mesh['grp'=4,'sp'=8] {'sp'}, use_global_device_ids=true, to_apply=%region_9.10 | all-reduce | flops 1 | bytes 8 | tf_op jit(solution)/shard_map/pmax | solution.py:92
  375.3 19.0 %all-to-all-done.4 = bf16[4,8,32,4096]{3,2,0,1:T(8,128)(2,1)} async-done(((bf16[4,8,32,4096]{3,2,0,1:T(8,128)(2,1)}), bf16[4,8,32,4096]{3,2,0,1:T(8,128)(2,1)}, u32[]{:S(2)}, u32[]{:S(2)}) %all-to-all-start.4) | async-done | bytes 8388640 | tf_op jit(solution)/shard_map/all_to_all | solution.py:110
  394.3 7.7 %copy.72 = bf16[4,8,32,4096]{3,2,1,0:T(8,128)(2,1)} copy(bf16[4,8,32,4096]{3,2,0,1:T(8,128)(2,1)} %all-to-all-done.4) | data formatting | bytes 16777216 | tf_op jit(solution)/shard_map/all_to_all | solution.py:110
  402.0 10.9 %fusion.1 = f32[1024,768]{1,0:T(8,128)S(1)} fusion(bf16[1024,4096]{1,0:T(8,128)(2,1)} %bitcast.86, bf16[1,4096,768]{2,1,0:T(8,128)(2,1)} %param.17), kind=kOutput, calls=%fused_computation.1 | convolution fusion | flops 6442450944 | bytes 17825792 | tf_op jit(solution)/shard_map/dot_general | solution.py:15
  412.9 1.4 fusion.19
  (15 shorter events, 0.1 us)
Async XLA Ops:
  8.4 13.6 %all-to-all-start = ((s32[64,8,1]{0,2,1:T(1,128)}), s32[64,8,1]{0,2,1:T(1,128)S(1)}, u32[]{:S(2)}, u32[]{:S(2)}) async-start(s32[64,8,1]{0,2,1:T(1,128)} %broadcast_in_dim.54), calls=%async_computation | async-start | bytes 8192 | tf_op jit(solution)/shard_map/all_to_all | solution.py:48
  22.1 16.8 %all-to-all-start.2 = ((bf16[64,8,512]{2,0,1:T(8,128)(2,1)}), bf16[64,8,512]{2,0,1:T(8,128)(2,1)S(1)}, u32[]{:S(2)}, u32[]{:S(2)}) async-start(bf16[64,8,512]{2,0,1:T(8,128)(2,1)} %bitcast.82), calls=%async_computation.2 | async-start | bytes 1048576 | tf_op jit(solution)/shard_map/all_to_all | solution.py:46
  39.5 12.0 %all-to-all-start.1 = ((bf16[64,8,256]{2,0,1:T(8,128)(2,1)}), bf16[64,8,256]{2,0,1:T(8,128)(2,1)S(1)}, u32[]{:S(2)}, u32[]{:S(2)}) async-start(bf16[64,8,256]{2,0,1:T(8,128)(2,1)} %bitcast.3), calls=%async_computation.1 | async-start | bytes 524288 | tf_op jit(solution)/shard_map/all_to_all | solution.py:47
  43.2 104.9 %reduce-scatter.2.cloned.1.call-start = ((), (), s32[]{:S(2)}) async-start(), calls=%async_computation.6 | async-start | bytes 4718592 | tf_op jit(solution)/shard_map/reduce_scatter | solution.py:81
  54.4 2.2 copy-start.1
  60.9 0.7 copy-start.4
  60.9 2.7 copy-start.5
  60.9 87.1 %copy-start.2 = (bf16[64,4096]{1,0:T(8,128)(2,1)S(1)}, bf16[64,4096]{1,0:T(8,128)(2,1)}, u32[]{:S(2)}) copy-start(bf16[64,4096]{1,0:T(8,128)(2,1)} %param.9) | copy-start | bytes 1572868
  60.9 88.5 %copy-start.3 = (f32[4096]{0:T(1024)S(1)}, f32[4096]{0:T(1024)}, u32[]{:S(2)}) copy-start(f32[4096]{0:T(1024)} %param.13) | copy-start | bytes 49156
  149.4 61.9 %copy-start = (bf16[64,4096]{1,0:T(8,128)(2,1)}, bf16[64,4096]{1,0:T(8,128)(2,1)S(1)}, u32[]{:S(2)}) copy-start(bf16[64,4096]{1,0:T(8,128)(2,1)S(1)} %get-tuple-element.20) | copy-start | bytes 1572868
  206.3 188.0 %all-to-all-start.4 = ((bf16[4,8,32,4096]{3,2,0,1:T(8,128)(2,1)}), bf16[4,8,32,4096]{3,2,0,1:T(8,128)(2,1)}, u32[]{:S(2)}, u32[]{:S(2)}) async-start(bf16[4,8,32,4096]{3,2,0,1:T(8,128)(2,1)} %bitcast.84), calls=%async_computation.5 | async-start | bytes 16777216 | tf_op jit(solution)/shard_map/all_to_all | solution.py:110
Sparse Core Ops, SparseCore 0:
  61.1 86.9 reduce-scatter.1
where the time goes:
time: 429 us; the launch traced here: 421 us
  blocking collectives  214 us (50%)
  waiting for transfers between devices  126 us (29%)
  local copies, waits for them, and re-layouts  20.9 us (5%)
  starting transfers between devices  19.4 us (5%)
  matrix products  18 us (4%)
  between operations  14.9 us (3%)
  other arithmetic  7.56 us (2%)
    pmax x1, blocking collectives, per_device(): group_amax = lax.pmax(jnp.max(jnp.abs(normed)).reshape(1), 'sp')  163 us
    reduce_scatter x1, waiting for transfers between devices, per_device(): lax.psum_scatter(jnp.dot(context, out_weight, preferred_element_type=jnp....  82.7 us
    all_to_all x1, blocking collectives, per_device(): lax.all_to_all(outgoing, 'grp', split_axis=0, concat_axis=0, tiled=True)  50.7 us
    all_to_all x1, waiting for transfers between devices, per_device(): lax.all_to_all(copies, 'sp', split_axis=1, concat_axis=1, tiled=True)  19 us
    all_to_all x1, waiting for transfers between devices, per_device(): lax.all_to_all(query_local, 'sp', split_axis=1, concat_axis=0, tiled=True)  12.3 us
    dot_general x1, matrix products, activate(): gate_up = jnp.dot(rows, weight, preferred_element_type=jnp.float32)  10.9 us
  transfers between devices with their start and end apart: 5, of which 5 were waited for; matrix products, arithmetic and copies ran while one was open for 2% of the time, Pallas kernels for 0%

commit v1 on v0

--- a/solution.py
+++ b/solution.py
@@ -1,6 +1,8 @@
 import jax
 import jax.numpy as jnp
 from jax import lax
+from jax.experimental import pallas as pl
+from jax.experimental.pallas import tpu as pltpu
 from jax.sharding import PartitionSpec as P
 
 QUERY_HEAD_SLICE = 32
@@ -16,6 +18,353 @@
     gate = gate_up[:, :width] * unscale
     upward = gate_up[:, width:] * unscale
     return (jax.nn.silu(gate) * upward).astype(jnp.bfloat16)
+
+
+def copy_to(source, target, send, receive, device):
+    return pltpu.make_async_remote_copy(
+        src_ref=source,
+        dst_ref=target,
+        send_sem=send,
+        recv_sem=receive,
+        device_id=device,
+        device_id_type=pl.DeviceIdType.MESH,
+    )
+
+
+def back_kernel(
+    context_ref,
+    residual_ref,
+    gain_ref,
+    history_ref,
+    pick_ref,
+    out_weight_ref,
+    expert_weight_ref,
+    after_ref,
+    hidden_ref,
+    amax_ref,
+    out_weight,
+    expert_weight,
+    pair_send,
+    pair_receive,
+    line_send,
+    line_receive,
+    rows,
+    amaxes,
+    local_sem,
+    pair_sems,
+    line_send_sems,
+    line_receive_sems,
+    row_send_sems,
+    row_receive_sems,
+    amax_send_sems,
+    amax_receive_sems,
+):
+    grp, sp = lax.axis_index("grp"), lax.axis_index("sp")
+    y, core = grp // 2, grp % 2
+    z, x = sp // 2, sp % 2
+    tokens, model = residual_ref.shape
+    chunks, _, chunk = pair_send.shape
+    width = hidden_ref.shape[1]
+    most = pick_ref.shape[1]
+
+    def device(x, y, core, z):
+        return (2 * y + core, 2 * z + x)
+
+    def slot(x, y, core, z):
+        return ((y * 2 + x) * 2 + core) * 4 + z
+
+    def block(place):
+        return rows.at[pl.ds(pl.multiple_of(place * tokens, tokens), tokens)]
+
+    def z_peer(step):
+        return lax.rem(z + step, 4)
+
+    sibling = device(x, y, 1 - core, z)
+    x_peer = device(1 - x, y, core, z)
+    y_peer = device(x, 1 - y, core, z)
+
+    def weight_chunk(k):
+        columns = pl.ds(pl.multiple_of(k * chunk, chunk), chunk)
+        return pltpu.make_async_copy(
+            out_weight_ref.at[:, columns], out_weight.at[k], local_sem.at[k]
+        )
+
+    expert_copy = pltpu.make_async_copy(expert_weight_ref, expert_weight, local_sem.at[chunks])
+    for k in range(chunks):
+        weight_chunk(k).start()
+    expert_copy.start()
+
+    barrier = pltpu.get_barrier_semaphore()
+    partners = [sibling, x_peer, y_peer]
+    for step in (1, 2, 3):
+        partners.append(device(x, y, core, z_peer(step)))
+        partners.append(device(1 - x, y, core, z_peer(step)))
+    for partner in partners:
+        pl.semaphore_signal(
+            barrier, inc=1, device_id=partner, device_id_type=pl.DeviceIdType.MESH
+        )
+    pl.semaphore_wait(barrier, len(partners))
+
+    def pair_copy(k):
+        return copy_to(
+            pair_send.at[k], pair_receive.at[k], pair_sems.at[0, k], pair_sems.at[1, k], x_peer
+        )
+
+    def send_pair(k, carry):
+        weight_chunk(k).wait()
+        term = jnp.dot(context_ref[1 - x], out_weight[k], preferred_element_type=jnp.float32)
+        pair_send[k] = term.astype(jnp.bfloat16)
+        pair_copy(k).start()
+        return carry
+
+    lax.fori_loop(0, chunks, send_pair, 0)
+
+    def line_copy(k, step):
+        target = z_peer(step)
+        source = line_send.at[k, pl.ds(pl.multiple_of(target * tokens, tokens), tokens)]
+        return copy_to(
+            source,
+            line_receive.at[k, step - 1],
+            line_send_sems.at[k, step - 1],
+            line_receive_sems.at[k, step - 1],
+            device(x, y, core, target),
+        )
+
+    def send_line(k, carry):
+        term = jnp.dot(context_ref[x], out_weight[k], preferred_element_type=jnp.float32)
+        pair_copy(k).wait_recv()
+        line_send[k] = (term + pair_receive[k].astype(jnp.float32)).astype(jnp.bfloat16)
+        for step in (2, 1, 3):
+            line_copy(k, step).start()
+        return carry
+
+    lax.fori_loop(0, chunks, send_line, 0)
+
+    def finish(k, squares):
+        columns = pl.ds(pl.multiple_of(k * chunk, chunk), chunk)
+        total = line_send[k, pl.ds(pl.multiple_of(z * tokens, tokens), tokens)].astype(jnp.float32)
+        for step in (1, 3, 2):
+            line_copy(k, step).wait_recv()
+            total = total + line_receive[k, step - 1].astype(jnp.float32)
+        after = (residual_ref[:, columns].astype(jnp.float32) + total).astype(jnp.bfloat16)
+        after_ref[:, columns] = after
+        widened = after.astype(jnp.float32)
+        return squares + jnp.sum(widened * widened, axis=1, keepdims=True)
+
+    squares = lax.fori_loop(0, chunks, finish, jnp.zeros((tokens, 1), jnp.float32))
+    inverse = lax.rsqrt(squares / model + 1e-06)
+    scale = 448.0 / history_ref[grp]
+    own_rows = pl.ds(pl.multiple_of(slot(x, y, core, z) * tokens, tokens), tokens)
+
+    def normalize(k, highest):
+        columns = pl.ds(pl.multiple_of(k * chunk, chunk), chunk)
+        normed = after_ref[:, columns].astype(jnp.float32) * inverse * gain_ref[:, columns]
+        rows[own_rows, columns] = jnp.clip(normed * scale, -448.0, 448.0).astype(jnp.bfloat16)
+        return jnp.maximum(highest, jnp.max(jnp.abs(normed), axis=1, keepdims=True))
+
+    highest = lax.fori_loop(0, chunks, normalize, jnp.zeros((tokens, 1), jnp.float32))
+
+    started = []
+
+    def pass_on(place, target, half=None, landing=0):
+        source = block(place)
+        if half is not None:
+            source = source.at[pl.ds(half * (tokens // 2), tokens // 2)]
+        started.append(
+            copy_to(
+                source,
+                source,
+                row_send_sems.at[len(started)],
+                row_receive_sems.at[place, landing],
+                target,
+            )
+        )
+        started[-1].start()
+
+    def arrived(place, half=None, landing=0):
+        source = block(place)
+        if half is not None:
+            source = source.at[pl.ds(half * (tokens // 2), tokens // 2)]
+        copy_to(
+            source, source, row_send_sems.at[0], row_receive_sems.at[place, landing], sibling
+        ).wait_recv()
+
+    own = slot(x, y, core, z)
+    pass_on(own, x_peer)
+    pass_on(own, y_peer)
+    for step in (1, 3, 2):
+        pass_on(own, device(x, y, core, z_peer(step)))
+    pass_on(own, sibling)
+
+    amaxes[sp] = jnp.broadcast_to(jnp.max(highest, axis=0, keepdims=True), amaxes.shape[1:])
+
+    def amax_copy(step):
+        target = lax.rem(sp + step, 8)
+        return copy_to(
+            amaxes.at[sp],
+            amaxes.at[sp],
+            amax_send_sems.at[step - 1],
+            amax_receive_sems.at[step - 1],
+            (grp, target),
+        )
+
+    for step in range(1, 8):
+        amax_copy(step).start()
+
+    for step in (1, 3, 2):
+        place = slot(x, y, core, z_peer(step))
+        arrived(place)
+        pass_on(place, x_peer)
+        pass_on(place, y_peer)
+        pass_on(place, sibling)
+
+    expert_copy.wait()
+
+    def compute(index, carry):
+        other_core = lax.rem(core + index, 2)
+        other_x = lax.rem(x + index // 2, 2)
+        other_y = lax.rem(y + index // 4, 2)
+        first = pl.multiple_of(slot(other_x, other_y, other_core, 0) * tokens, 4 * tokens)
+        gate_up = jnp.dot(
+            rows[pl.ds(first, 4 * tokens)], expert_weight[...], preferred_element_type=jnp.float32
+        )
+        source = 2 * other_y + other_core
+        unscale = history_ref[source] / 448.0
+        gate = gate_up[:, :width] * unscale
+        upward = gate_up[:, width:] * unscale
+        hidden = (gate / (1.0 + jnp.exp(-gate)) * upward).astype(jnp.bfloat16)
+        for line in range(4):
+            origin = source * 8 + 2 * line + other_x
+            picked = jnp.dot(
+                pick_ref[origin],
+                hidden[line * tokens : (line + 1) * tokens],
+                preferred_element_type=jnp.float32,
+            )
+            hidden_ref[pl.ds(pl.multiple_of(origin * most, most), most)] = picked.astype(
+                jnp.bfloat16
+            )
+        return carry
+
+    def sibling_group(x, y):
+        for line in range(4):
+            arrived(slot(x, y, 1 - core, line))
+
+    lax.fori_loop(0, 1, compute, 0)
+    sibling_group(x, y)
+    lax.fori_loop(1, 2, compute, 0)
+
+    for step in (0, 1, 3, 2):
+        place = slot(1 - x, y, core, z_peer(step))
+        arrived(place)
+        pass_on(place, y_peer, 0, 0)
+        pass_on(place, sibling)
+        place = slot(x, 1 - y, core, z_peer(step))
+        arrived(place)
+        pass_on(place, x_peer, 1, 1)
+        pass_on(place, sibling)
+    sibling_group(1 - x, y)
+    sibling_group(x, 1 - y)
+    lax.fori_loop(2, 6, compute, 0)
+
+    for step in (0, 1, 3, 2):
+        place = slot(1 - x, 1 - y, core, z_peer(step))
+        arrived(place, 0, 0)
+        arrived(place, 1, 1)
+        pass_on(place, sibling)
+    lax.fori_loop(6, 7, compute, 0)
+    sibling_group(1 - x, 1 - y)
+    lax.fori_loop(7, 8, compute, 0)
+
+    for step in range(1, 8):
+        amax_copy(step).wait_recv()
+    amax_ref[...] = jnp.max(amaxes[...], axis=0)
+
+    for step in range(1, 8):
+        amax_copy(step).wait_send()
+    for copy in started:
+        copy.wait_send()
+
+    def drain(k, carry):
+        pair_copy(k).wait_send()
+        for step in (1, 2, 3):
+            line_copy(k, step).wait_send()
+        return carry
+
+    lax.fori_loop(0, chunks, drain, 0)
+
+
+def back(context, residual, norm_gain, amax_history, picks, out_weight, expert_weight):
+    tokens, model = residual.shape
+    block_width = out_weight.shape[0]
+    width = expert_weight.shape[1] // 2
+    devices, most, _ = picks.shape
+    chunks = 8
+    chunk = model // chunks
+    vmem = pl.BlockSpec(memory_space=pltpu.VMEM)
+    smem = pl.BlockSpec(memory_space=pltpu.SMEM)
+    hbm = pl.BlockSpec(memory_space=pl.ANY)
+    dma = pltpu.SemaphoreType.DMA
+    halves = jnp.transpose(context.reshape(4, 2, tokens, block_width), (1, 0, 2, 3))
+    return pl.pallas_call(
+        back_kernel,
+        out_shape=(
+            jax.ShapeDtypeStruct((tokens, model), jnp.bfloat16),
+            jax.ShapeDtypeStruct((devices * most, width), jnp.bfloat16),
+            jax.ShapeDtypeStruct((8, 128), jnp.float32),
+        ),
+        in_specs=[vmem, vmem, vmem, smem, vmem, hbm, hbm],
+        out_specs=(vmem, vmem, vmem),
+        scratch_shapes=[
+            pltpu.VMEM((chunks, block_width, chunk), jnp.bfloat16),
+            pltpu.VMEM(expert_weight.shape, jnp.bfloat16),
+            pltpu.VMEM((chunks, 4 * tokens, chunk), jnp.bfloat16),
+            pltpu.VMEM((chunks, 4 * tokens, chunk), jnp.bfloat16),
+            pltpu.VMEM((chunks, 4 * tokens, chunk), jnp.bfloat16),
+            pltpu.VMEM((chunks, 3, tokens, chunk), jnp.bfloat16),
+            pltpu.VMEM((devices * tokens, model), jnp.bfloat16),
+            pltpu.VMEM((8, 8, 128), jnp.float32),
+            dma((chunks + 1,)),
+            dma((2, chunks)),
+            dma((chunks, 3)),
+            dma((chunks, 3)),
+            dma((35,)),
+            dma((devices, 2)),
+            dma((7,)),
+            dma((7,)),
+        ],
+        compiler_params=pltpu.CompilerParams(
+            collective_id=0, has_side_effects=True, vmem_limit_bytes=56 * 1024 * 1024
+        ),
+        cost_estimate=pl.CostEstimate(
+            flops=2 * devices * tokens * model * 2 * width,
+            bytes_accessed=12 * 1024 * 1024,
+            transcendentals=devices * tokens * width,
+        ),
+        name="project_norm_dispatch",
+    )(
+        halves.reshape(2, 4 * tokens, block_width),
+        residual,
+        norm_gain.reshape(1, model),
+        amax_history,
+        picks,
+        out_weight,
+        expert_weight,
+    )
+
+
+def pick_rows(expert_ids, most_rows):
+    local_row_count = expert_ids.shape[0]
+    everyone = lax.all_gather(expert_ids, ("grp", "sp"), axis=0)
+    expert = (
+        lax.axis_index("grp") * (lax.axis_size("sp") // HALVES) + lax.axis_index("sp") // HALVES
+    )
+    named = jnp.any(everyone == expert, axis=2)
+    order = jnp.arange(local_row_count, dtype=jnp.int32)
+    earlier = (order[:, None] < order[None, :]).astype(jnp.bfloat16)
+    rank = jnp.dot(named.astype(jnp.bfloat16), earlier, preferred_element_type=jnp.float32)
+    slots = jnp.arange(most_rows, dtype=jnp.int32)
+    chosen = named[:, None, :] & (rank.astype(jnp.int32)[:, None, :] == slots[None, :, None])
+    return chosen.astype(jnp.bfloat16)
 
 
 def per_device(
@@ -78,6 +427,19 @@
     context = lax.map(attend, jnp.arange(slice_length // block_rows, dtype=jnp.int32))
     block_width = heads_here * HEAD_SIZE
     context = context.reshape(slice_length, block_width)
+    experts = grp_count * sequence_parallel_count // HALVES
+    most_rows = max(2, local_row_count * TOP // experts)
+    if (grp_count, sequence_parallel_count) == (4, 8):
+        after_attention, expert_hidden, highest = back(
+            context,
+            residual,
+            norm_gain,
+            amax_history,
+            pick_rows(expert_ids, most_rows),
+            out_weight,
+            gate_up_weight[0],
+        )
+        return after_attention, expert_hidden[None], highest[0, :1]
     projected = lax.psum_scatter(
         jnp.dot(context, out_weight, preferred_element_type=jnp.float32).astype(jnp.bfloat16),
         "sp",
@@ -92,8 +454,6 @@
     group_amax = lax.pmax(jnp.max(jnp.abs(normed)).reshape(1), "sp")
     own_history = lax.dynamic_index_in_dim(amax_history, lax.axis_index("grp"), 0, False)
     quantized = jnp.clip(normed * (448.0 / own_history), -448.0, 448.0).astype(jnp.bfloat16)
-    experts = grp_count * sequence_parallel_count // HALVES
-    most_rows = max(2, local_row_count * TOP // experts)
     routing = expert_ids.reshape(local_row_count * TOP)
     one_hot = (routing[:, None] == jnp.arange(experts, dtype=jnp.int32)[None, :]).astype(jnp.int32)
     rank = jnp.sum((jnp.cumsum(one_hot, axis=0) - one_hot) * one_hot, axis=1)

time: 429 us -> 259 us (0.60); the launches traced: 421 us -> 258 us
  Pallas kernels: 0 us -> 146 us
  blocking collectives: 214 us -> 69 us
  waiting for transfers between devices: 126 us -> 11.4 us
  matrix products: 18 us -> 1.62 us
  between operations: 14.9 us -> 0.74 us
  local copies, waits for them, and re-layouts: 20.9 us -> 11.6 us
  starting transfers between devices: 19.4 us -> 14.2 us
  other arithmetic: 7.56 us -> 3.23 us
    pmax x1 -> x0, blocking collectives: 163 us -> none  [per_device(): group_amax = lax.pmax(jnp.max(jnp.abs(normed)).reshape(1), 'sp')]
    pallas_call x0 -> x1, Pallas kernels: none -> 146 us  [back(): pl.pallas_call(back_kernel, out_shape=(jax.ShapeDtypeStruct((tokens, mode...]
    reduce_scatter x1 -> x0, waiting for transfers between devices: 82.7 us -> none  [per_device(): lax.psum_scatter(jnp.dot(context, out_weight, preferred_element_type=jnp....]
    all_gather x0 -> x1, blocking collectives: none -> 69 us  [pick_rows(): everyone = lax.all_gather(expert_ids, ('grp', 'sp'), axis=0)]
    all_to_all x1 -> x0, blocking collectives: 50.7 us -> none  [per_device(): lax.all_to_all(outgoing, 'grp', split_axis=0, concat_axis=0, tiled=True)]
    all_to_all x1 -> x0, waiting for transfers between devices: 19 us -> none  [per_device(): lax.all_to_all(copies, 'sp', split_axis=1, concat_axis=1, tiled=True)]
    dot_general x3 -> x1, matrix products: 16.5 us -> 0.13 us  [pick_rows(): jnp.dot(named.astype(jnp.bfloat16), earlier, preferred_element_type=jnp.f...]
    all_to_all x1, waiting for transfers between devices: 12.3 us -> 0.01 us  [per_device(): lax.all_to_all(query_local, 'sp', split_axis=1, concat_axis=0, tiled=True)]
  transfers between devices with their start and end apart: 5 -> 3, of which waited for: 5 -> 2; matrix products, arithmetic and copies ran while one was open for 2% -> 2% of each run, Pallas kernels for 0% -> 0%
where the time goes in v1:
time: 259 us; the launch traced here: 258 us
  Pallas kernels  146 us (56%)
  blocking collectives  69 us (27%)
  starting transfers between devices  14.2 us (5%)
  local copies, waits for them, and re-layouts  11.6 us (4%)
  waiting for transfers between devices  11.4 us (4%)
  other arithmetic  3.23 us (1%)
    pallas_call x1, Pallas kernels, back(): pl.pallas_call(back_kernel, out_shape=(jax.ShapeDtypeStruct((tokens, mode...  146 us
    all_gather x1, blocking collectives, pick_rows(): everyone = lax.all_gather(expert_ids, ('grp', 'sp'), axis=0)  69 us
    all_to_all x1, starting transfers between devices, per_device(): lax.all_to_all(doc_copies, 'sp', split_axis=1, concat_axis=0, tiled=True)  7.25 us
    all_to_all x1, waiting for transfers between devices, per_device(): lax.all_to_all(pair_replicas, 'sp', split_axis=1, concat_axis=0, tiled=True)  6.92 us
  transfers between devices with their start and end apart: 3, of which 2 were waited for; matrix products, arithmetic and copies ran while one was open for 2% of the time, Pallas kernels for 0%

profile of v1, /device:TPU:0, one launch (start us, length us, event | category | flops | bytes accessed | tf_op | source)
XLA Modules:
  0.0 257.6 jit_solution(8537271431937204397)
XLA Ops:
  0.6 1.3 broadcast_in_dim.51
  1.9 7.3 %all-to-all-start = ((s32[64,8,1]{0,2,1:T(1,128)}), s32[64,8,1]{0,2,1:T(1,128)S(1)}, u32[]{:S(2)}, u32[]{:S(2)}) async-start(s32[64,8,1]{0,2,1:T(1,128)} %broadcast_in_dim.51), calls=%async_computation | async-start | bytes 8192 | tf_op jit(solution)/shard_map/all_to_all | solution.py:397
  9.1 1.9 copy.33
  11.0 4.5 %all-to-all-done = s32[64,8,1]{0,2,1:T(1,128)S(1)} async-done(((s32[64,8,1]{0,2,1:T(1,128)}), s32[64,8,1]{0,2,1:T(1,128)S(1)}, u32[]{:S(2)}, u32[]{:S(2)}) %all-to-all-start) | async-done | bytes 2080 | tf_op jit(solution)/shard_map/all_to_all | solution.py:397
  15.5 3.5 %all-to-all-start.2 = ((bf16[64,8,512]{2,0,1:T(8,128)(2,1)}), bf16[64,8,512]{2,0,1:T(8,128)(2,1)S(1)}, u32[]{:S(2)}, u32[]{:S(2)}) async-start(bf16[64,8,512]{2,0,1:T(8,128)(2,1)} %bitcast.54), calls=%async_computation.2 | async-start | bytes 1048576 | tf_op jit(solution)/shard_map/all_to_all | solution.py:395
  19.0 0.9 copy.34
  20.0 69.0 %all-gather.1 = s32[32,64,8]{1,2,0:T(8,128)S(1)} all-gather(s32[1,64,8]{1,2,0:T(8,128)} %bitcast.66), channel_id=2, replica_groups=mesh['grp'=4,'sp'=8] {'grp','sp'}, dimensions={0}, use_global_device_ids=true | all-gather | bytes 67584 | tf_op jit(solution)/shard_map/all_gather | solution.py:357
  89.0 0.1 compare_reduce_fusion
  89.0 0.1 convolution_convert_fusion
  89.2 0.0 all-to-all-done.2
  89.2 0.7 broadcast_in_dim.53
  89.9 3.4 %all-to-all-start.1 = ((bf16[64,8,256]{2,0,1:T(8,128)(2,1)}), bf16[64,8,256]{2,0,1:T(8,128)(2,1)S(1)}, u32[]{:S(2)}, u32[]{:S(2)}) async-start(bf16[64,8,256]{2,0,1:T(8,128)(2,1)} %bitcast.3), calls=%async_computation.1 | async-start | bytes 524288 | tf_op jit(solution)/shard_map/all_to_all | solution.py:396
  93.3 0.8 fusion.12.pick_ref
  94.1 0.1 eq.45
  94.2 0.2 fusion.8
  94.4 0.1 reshape.97
  94.5 6.9 %all-to-all-done.1 = bf16[64,8,256]{2,0,1:T(8,128)(2,1)S(1)} async-done(((bf16[64,8,256]{2,0,1:T(8,128)(2,1)}), bf16[64,8,256]{2,0,1:T(8,128)(2,1)S(1)}, u32[]{:S(2)}, u32[]{:S(2)}) %all-to-all-start.1) | async-done | bytes 262176 | tf_op jit(solution)/shard_map/all_to_all | solution.py:396
  101.5 0.7 fusion.9
  102.2 2.1 fusion.15
  104.3 0.8 fusion.7
  105.1 0.4 copy.24
  105.5 0.2 reshape_reshape.3
  105.7 0.8 copy.25
  106.6 145.8 %project_norm_dispatch.1 = (bf16[64,4096]{1,0:T(8,128)(2,1)}, bf16[1024,384]{1,0:T(8,128)(2,1)}, f32[8,128]{1,0:T(8,128)}) custom-call(bf16[2,256,512]{2,1,0:T(8,128)(2,1)} %bitcast.63, bf16[64,4096]{1,0:T(8,128)(2,1)} %residual_ref.1, f32[1,4096]{1,0:T(1,128)} %bitcast.69, f32[4]{0:T(128)} %history_ref.1, bf16[32,32,64]{2,1,0:T(8,128)(2,1)} %fusion.12.pick_ref, ...), custom_call_target="tpu_custom_call" | custom-call | flops 12884901888 | bytes 12582912 | tf_op jit(solution)/shard_map/project_norm_dispatch/pallas_call | solution.py:308
  252.4 1.2 slice.11
  253.6 1.9 copy.37
  255.5 2.1 copy.38
Async XLA Ops:
  1.9 13.6 %all-to-all-start = ((s32[64,8,1]{0,2,1:T(1,128)}), s32[64,8,1]{0,2,1:T(1,128)S(1)}, u32[]{:S(2)}, u32[]{:S(2)}) async-start(s32[64,8,1]{0,2,1:T(1,128)} %broadcast_in_dim.51), calls=%async_computation | async-start | bytes 8192 | tf_op jit(solution)/shard_map/all_to_all | solution.py:397
  15.5 73.6 %all-to-all-start.2 = ((bf16[64,8,512]{2,0,1:T(8,128)(2,1)}), bf16[64,8,512]{2,0,1:T(8,128)(2,1)S(1)}, u32[]{:S(2)}, u32[]{:S(2)}) async-start(bf16[64,8,512]{2,0,1:T(8,128)(2,1)} %bitcast.54), calls=%async_computation.2 | async-start | bytes 1048576 | tf_op jit(solution)/shard_map/all_to_all | solution.py:395
  89.9 11.6 %all-to-all-start.1 = ((bf16[64,8,256]{2,0,1:T(8,128)(2,1)}), bf16[64,8,256]{2,0,1:T(8,128)(2,1)S(1)}, u32[]{:S(2)}, u32[]{:S(2)}) async-start(bf16[64,8,256]{2,0,1:T(8,128)(2,1)} %bitcast.3), calls=%async_computation.1 | async-start | bytes 524288 | tf_op jit(solution)/shard_map/all_to_all | solution.py:396

commit v2 on v1

--- a/solution.py
+++ b/solution.py
@@ -31,17 +31,23 @@
     )
 
 
-def back_kernel(
-    context_ref,
+def layer_kernel(
+    queries_ref,
+    pairs_ref,
+    documents_ref,
     residual_ref,
     gain_ref,
     history_ref,
-    pick_ref,
+    ranks_ref,
     out_weight_ref,
     expert_weight_ref,
     after_ref,
     hidden_ref,
     amax_ref,
+    query_rows,
+    pair_rows,
+    pair_blocks,
+    context,
     out_weight,
     expert_weight,
     pair_send,
@@ -58,6 +64,8 @@
     row_receive_sems,
     amax_send_sems,
     amax_receive_sems,
+    head_send_sems,
+    head_receive_sems,
 ):
     grp, sp = lax.axis_index("grp"), lax.axis_index("sp")
     y, core = grp // 2, grp % 2
@@ -65,7 +73,9 @@
     tokens, model = residual_ref.shape
     chunks, _, chunk = pair_send.shape
     width = hidden_ref.shape[1]
-    most = pick_ref.shape[1]
+    most = hidden_ref.shape[0] * tokens // rows.shape[0]
+    heads_width = query_rows.shape[1]
+    nearest = (z, z + 1 - 2 * (z % 2), 2 - z // 2, 3 * (1 - z // 2))
 
     def device(x, y, core, z):
         return (2 * y + core, 2 * z + x)
@@ -93,6 +103,12 @@
     for k in range(chunks):
         weight_chunk(k).start()
     expert_copy.start()
+
+    for head in range(KEY_VALUE_HEADS):
+        pair_blocks[head, :, : 2 * HEAD_SIZE] = pairs_ref[
+            :, head * 2 * HEAD_SIZE : (head + 1) * 2 * HEAD_SIZE
+        ]
+        pair_blocks[head, :, 2 * HEAD_SIZE :] = documents_ref[...]
 
     barrier = pltpu.get_barrier_semaphore()
     partners = [sibling, x_peer, y_peer]
@@ -105,6 +121,89 @@
         )
     pl.semaphore_wait(barrier, len(partners))
 
+    def token_rows(member):
+        place = (member % 2) * 4 + member // 2
+        return pl.ds(pl.multiple_of(place * tokens, tokens), tokens)
+
+    def query_columns(member):
+        return queries_ref.at[
+            :, pl.ds(pl.multiple_of(member * heads_width, heads_width), heads_width)
+        ]
+
+    def head_copies(step, origin):
+        target = lax.rem(sp + step, 8)
+        return (
+            copy_to(
+                pair_blocks.at[target // 2],
+                pair_rows.at[token_rows(origin)],
+                head_send_sems.at[0, step - 1],
+                head_receive_sems.at[0, step - 1],
+                (grp, target),
+            ),
+            copy_to(
+                query_columns(target),
+                query_rows.at[token_rows(origin)],
+                head_send_sems.at[1, step - 1],
+                head_receive_sems.at[1, step - 1],
+                (grp, target),
+            ),
+        )
+
+    for step in range(1, 8):
+        for copy in head_copies(step, sp):
+            copy.start()
+    own_queries = pltpu.make_async_copy(
+        query_columns(sp), query_rows.at[token_rows(sp)], local_sem.at[chunks + 1]
+    )
+    own_queries.start()
+    pair_rows[token_rows(sp)] = pair_blocks[sp // 2]
+    own_queries.wait()
+    for step in range(1, 8):
+        for copy in head_copies(step, lax.rem(sp + 8 - step, 8)):
+            copy.wait_recv()
+
+    def attend(half):
+        count = 4 * tokens
+        here = pl.ds(pl.multiple_of(half * count, count), count)
+        row = lax.broadcasted_iota(jnp.int32, (count, 1), 0)
+        column = lax.broadcasted_iota(jnp.int32, (1, 2 * count), 1)
+        row_position = (lax.div(row, tokens) * 2 + half) * tokens + lax.rem(row, tokens)
+        column_half = lax.div(column, count)
+        column_place = lax.rem(column, count)
+        column_position = (lax.div(column_place, tokens) * 2 + column_half) * tokens + lax.rem(
+            column_place, tokens
+        )
+        lanes = slice(2 * HEAD_SIZE, 3 * HEAD_SIZE)
+        first_lane = lax.broadcasted_iota(jnp.int32, (16, HEAD_SIZE), 1) == 0
+        column_documents = lax.dot_general(
+            first_lane.astype(jnp.bfloat16),
+            pair_rows[:, lanes],
+            (((1,), (1,)), ((), ())),
+            preferred_element_type=jnp.float32,
+        )[:1]
+        row_documents = pair_rows[here, lanes].astype(jnp.float32)[:, :1]
+        allowed = (column_position <= row_position) & (row_documents == column_documents)
+
+        def one_head(head, carry):
+            columns = pl.ds(pl.multiple_of(head * HEAD_SIZE, HEAD_SIZE), HEAD_SIZE)
+            scores = lax.dot_general(
+                query_rows[here, columns],
+                pair_rows[:, :HEAD_SIZE],
+                (((1,), (1,)), ((), ())),
+                preferred_element_type=jnp.float32,
+            ) * HEAD_SIZE ** (-0.5)
+            scores = jnp.where(allowed, scores, -jnp.inf)
+            weights = jnp.exp(scores - jnp.max(scores, axis=1, keepdims=True))
+            probs = (weights / jnp.sum(weights, axis=1, keepdims=True)).astype(jnp.bfloat16)
+            context[half, :, columns] = jnp.dot(
+                probs, pair_rows[:, HEAD_SIZE : 2 * HEAD_SIZE], preferred_element_type=jnp.float32
+            ).astype(jnp.bfloat16)
+            return carry
+
+        lax.fori_loop(0, heads_width // HEAD_SIZE, one_head, 0)
+
+    attend(1 - x)
+
     def pair_copy(k):
         return copy_to(
             pair_send.at[k], pair_receive.at[k], pair_sems.at[0, k], pair_sems.at[1, k], x_peer
@@ -112,12 +211,13 @@
 
     def send_pair(k, carry):
         weight_chunk(k).wait()
-        term = jnp.dot(context_ref[1 - x], out_weight[k], preferred_element_type=jnp.float32)
+        term = jnp.dot(context[1 - x], out_weight[k], preferred_element_type=jnp.float32)
         pair_send[k] = term.astype(jnp.bfloat16)
         pair_copy(k).start()
         return carry
 
     lax.fori_loop(0, chunks, send_pair, 0)
+    attend(x)
 
     def line_copy(k, step):
         target = z_peer(step)
@@ -131,7 +231,7 @@
         )
 
     def send_line(k, carry):
-        term = jnp.dot(context_ref[x], out_weight[k], preferred_element_type=jnp.float32)
+        term = jnp.dot(context[x], out_weight[k], preferred_element_type=jnp.float32)
         pair_copy(k).wait_recv()
         line_send[k] = (term + pair_receive[k].astype(jnp.float32)).astype(jnp.bfloat16)
         for step in (2, 1, 3):
@@ -164,22 +264,30 @@
 
     highest = lax.fori_loop(0, chunks, normalize, jnp.zeros((tokens, 1), jnp.float32))
 
+    rows[own_rows, pl.ds(model, 128)] = ranks_ref[...]
+
     started = []
 
-    def pass_on(place, target, half=None, landing=0):
-        source = block(place)
-        if half is not None:
-            source = source.at[pl.ds(half * (tokens // 2), tokens // 2)]
-        started.append(
-            copy_to(
+    def pass_on(place, target, half=None, landing=0, allowed=None):
+        number = len(started)
+
+        def describe():
+            source = block(place)
+            if half is not None:
+                source = source.at[pl.ds(half * (tokens // 2), tokens // 2)]
+            return copy_to(
                 source,
                 source,
-                row_send_sems.at[len(started)],
+                row_send_sems.at[number],
                 row_receive_sems.at[place, landing],
                 target,
             )
-        )
-        started[-1].start()
+
+        started.append((describe, allowed))
+        if allowed is None:
+            describe().start()
+        else:
+            pl.when(allowed)(lambda: describe().start())
 
     def arrived(place, half=None, landing=0):
         source = block(place)
@@ -192,8 +300,8 @@
     own = slot(x, y, core, z)
     pass_on(own, x_peer)
     pass_on(own, y_peer)
-    for step in (1, 3, 2):
-        pass_on(own, device(x, y, core, z_peer(step)))
+    pass_on(own, device(x, y, core, z + 1), allowed=z < 3)
+    pass_on(own, device(x, y, core, z - 1), allowed=z > 0)
     pass_on(own, sibling)
 
     amaxes[sp] = jnp.broadcast_to(jnp.max(highest, axis=0, keepdims=True), amaxes.shape[1:])
@@ -211,14 +319,20 @@
     for step in range(1, 8):
         amax_copy(step).start()
 
-    for step in (1, 3, 2):
-        place = slot(x, y, core, z_peer(step))
+    for order in (1, 2, 3):
+        place = slot(x, y, core, nearest[order])
         arrived(place)
+        onward = 3 - z if order == 1 else 3 * (z - 1)
+        pass_on(place, device(x, y, core, onward), allowed=z * (3 - z) > 0)
         pass_on(place, x_peer)
         pass_on(place, y_peer)
         pass_on(place, sibling)
 
     expert_copy.wait()
+    expert = grp * 4 + z
+    expert_lane = lax.broadcasted_iota(jnp.int32, (most, 128), 1) == expert
+    expert_lane = expert_lane.astype(jnp.bfloat16)
+    slots = lax.broadcasted_iota(jnp.int32, (most, tokens), 0)
 
     def compute(index, carry):
         other_core = lax.rem(core + index, 2)
@@ -226,7 +340,9 @@
         other_y = lax.rem(y + index // 4, 2)
         first = pl.multiple_of(slot(other_x, other_y, other_core, 0) * tokens, 4 * tokens)
         gate_up = jnp.dot(
-            rows[pl.ds(first, 4 * tokens)], expert_weight[...], preferred_element_type=jnp.float32
+            rows[pl.ds(first, 4 * tokens), pl.ds(0, model)],
+            expert_weight[...],
+            preferred_element_type=jnp.float32,
         )
         source = 2 * other_y + other_core
         unscale = history_ref[source] / 448.0
@@ -235,8 +351,14 @@
         hidden = (gate / (1.0 + jnp.exp(-gate)) * upward).astype(jnp.bfloat16)
         for line in range(4):
             origin = source * 8 + 2 * line + other_x
+            ranks = lax.dot_general(
+                expert_lane,
+                rows[pl.ds(pl.multiple_of(first + line * tokens, tokens), tokens), pl.ds(model, 128)],
+                (((1,), (1,)), ((), ())),
+                preferred_element_type=jnp.float32,
+            )
             picked = jnp.dot(
-                pick_ref[origin],
+                (ranks.astype(jnp.int32) == slots).astype(jnp.bfloat16),
                 hidden[line * tokens : (line + 1) * tokens],
                 preferred_element_type=jnp.float32,
             )
@@ -253,12 +375,12 @@
     sibling_group(x, y)
     lax.fori_loop(1, 2, compute, 0)
 
-    for step in (0, 1, 3, 2):
-        place = slot(1 - x, y, core, z_peer(step))
+    for line in nearest:
+        place = slot(1 - x, y, core, line)
         arrived(place)
         pass_on(place, y_peer, 0, 0)
         pass_on(place, sibling)
-        place = slot(x, 1 - y, core, z_peer(step))
+        place = slot(x, 1 - y, core, line)
         arrived(place)
         pass_on(place, x_peer, 1, 1)
         pass_on(place, sibling)
@@ -266,8 +388,8 @@
     sibling_group(x, 1 - y)
     lax.fori_loop(2, 6, compute, 0)
 
-    for step in (0, 1, 3, 2):
-        place = slot(1 - x, 1 - y, core, z_peer(step))
+    for line in nearest:
+        place = slot(1 - x, 1 - y, core, line)
         arrived(place, 0, 0)
         arrived(place, 1, 1)
         pass_on(place, sibling)
@@ -281,8 +403,14 @@
 
     for step in range(1, 8):
         amax_copy(step).wait_send()
-    for copy in started:
-        copy.wait_send()
+    for describe, allowed in started:
+        if allowed is None:
+            describe().wait_send()
+        else:
+            pl.when(allowed)(lambda describe=describe: describe().wait_send())
+    for step in range(1, 8):
+        for copy in head_copies(step, sp):
+            copy.wait_send()
 
     def drain(k, carry):
         pair_copy(k).wait_send()
@@ -293,44 +421,61 @@
     lax.fori_loop(0, chunks, drain, 0)
 
 
-def back(context, residual, norm_gain, amax_history, picks, out_weight, expert_weight):
+def whole_layer(
+    queries,
+    key_value_pairs,
+    doc_ids,
+    residual,
+    norm_gain,
+    amax_history,
+    ranks,
+    out_weight,
+    expert_weight,
+    devices,
+    most,
+):
     tokens, model = residual.shape
     block_width = out_weight.shape[0]
     width = expert_weight.shape[1] // 2
-    devices, most, _ = picks.shape
     chunks = 8
     chunk = model // chunks
     vmem = pl.BlockSpec(memory_space=pltpu.VMEM)
     smem = pl.BlockSpec(memory_space=pltpu.SMEM)
     hbm = pl.BlockSpec(memory_space=pl.ANY)
     dma = pltpu.SemaphoreType.DMA
-    halves = jnp.transpose(context.reshape(4, 2, tokens, block_width), (1, 0, 2, 3))
+    documents = jnp.broadcast_to(doc_ids.reshape(tokens, 1).astype(jnp.bfloat16), (tokens, 128))
     return pl.pallas_call(
-        back_kernel,
+        layer_kernel,
         out_shape=(
             jax.ShapeDtypeStruct((tokens, model), jnp.bfloat16),
             jax.ShapeDtypeStruct((devices * most, width), jnp.bfloat16),
             jax.ShapeDtypeStruct((8, 128), jnp.float32),
         ),
-        in_specs=[vmem, vmem, vmem, smem, vmem, hbm, hbm],
+        in_specs=[hbm, vmem, vmem, vmem, vmem, smem, vmem, hbm, hbm],
         out_specs=(vmem, vmem, vmem),
         scratch_shapes=[
+            pltpu.VMEM((8 * tokens, block_width), jnp.bfloat16),
+            pltpu.VMEM((8 * tokens, 3 * HEAD_SIZE), jnp.bfloat16),
+            pltpu.VMEM((KEY_VALUE_HEADS, tokens, 3 * HEAD_SIZE), jnp.bfloat16),
+            pltpu.VMEM((2, 4 * tokens, block_width), jnp.bfloat16),
             pltpu.VMEM((chunks, block_width, chunk), jnp.bfloat16),
             pltpu.VMEM(expert_weight.shape, jnp.bfloat16),
             pltpu.VMEM((chunks, 4 * tokens, chunk), jnp.bfloat16),
             pltpu.VMEM((chunks, 4 * tokens, chunk), jnp.bfloat16),
             pltpu.VMEM((chunks, 4 * tokens, chunk), jnp.bfloat16),
             pltpu.VMEM((chunks, 3, tokens, chunk), jnp.bfloat16),
-            pltpu.VMEM((devices * tokens, model), jnp.bfloat16),
+            pltpu.VMEM((devices * tokens, model + 128), jnp.bfloat16),
             pltpu.VMEM((8, 8, 128), jnp.float32),
-            dma((chunks + 1,)),
+            dma((chunks + 2,)),
             dma((2, chunks)),
             dma((chunks, 3)),
             dma((chunks, 3)),
-            dma((35,)),
+            dma((40,)),
             dma((devices, 2)),
             dma((7,)),
             dma((7,)),
+            dma((2, 7)),
+            dma((2, 7)),
         ],
         compiler_params=pltpu.CompilerParams(
             collective_id=0, has_side_effects=True, vmem_limit_bytes=56 * 1024 * 1024
@@ -340,31 +485,28 @@
             bytes_accessed=12 * 1024 * 1024,
             transcendentals=devices * tokens * width,
         ),
-        name="project_norm_dispatch",
+        name="attend_project_norm_dispatch",
     )(
-        halves.reshape(2, 4 * tokens, block_width),
+        queries,
+        key_value_pairs,
+        documents,
         residual,
         norm_gain.reshape(1, model),
         amax_history,
-        picks,
+        ranks,
         out_weight,
         expert_weight,
     )
 
 
-def pick_rows(expert_ids, most_rows):
+def rank_table(expert_ids, experts):
     local_row_count = expert_ids.shape[0]
-    everyone = lax.all_gather(expert_ids, ("grp", "sp"), axis=0)
-    expert = (
-        lax.axis_index("grp") * (lax.axis_size("sp") // HALVES) + lax.axis_index("sp") // HALVES
-    )
-    named = jnp.any(everyone == expert, axis=2)
+    numbers = jnp.arange(128, dtype=jnp.int32)
+    named = jnp.any(expert_ids[:, :, None] == numbers[None, None, :], axis=1)
     order = jnp.arange(local_row_count, dtype=jnp.int32)
-    earlier = (order[:, None] < order[None, :]).astype(jnp.bfloat16)
-    rank = jnp.dot(named.astype(jnp.bfloat16), earlier, preferred_element_type=jnp.float32)
-    slots = jnp.arange(most_rows, dtype=jnp.int32)
-    chosen = named[:, None, :] & (rank.astype(jnp.int32)[:, None, :] == slots[None, :, None])
-    return chosen.astype(jnp.bfloat16)
+    earlier = (order[None, :] < order[:, None]).astype(jnp.bfloat16)
+    rank = jnp.dot(earlier, named.astype(jnp.bfloat16), preferred_element_type=jnp.float32)
+    return jnp.where(named & (numbers < experts), rank, -1.0).astype(jnp.bfloat16)
 
 
 def per_device(
@@ -382,6 +524,23 @@
     grp_count = lax.axis_size("grp")
     local_row_count = residual.shape[0]
     heads_here = QUERY_HEAD_SLICE // sequence_parallel_count
+    experts = grp_count * sequence_parallel_count // HALVES
+    most_rows = max(2, local_row_count * TOP // experts)
+    if (grp_count, sequence_parallel_count) == (4, 8):
+        after_attention, expert_hidden, highest = whole_layer(
+            queries,
+            key_value_pairs,
+            doc_ids,
+            residual,
+            norm_gain,
+            amax_history,
+            rank_table(expert_ids, experts),
+            out_weight,
+            gate_up_weight[0],
+            grp_count * sequence_parallel_count,
+            most_rows,
+        )
+        return after_attention, expert_hidden[None], highest[0, :1]
     query_local = queries.reshape(local_row_count, sequence_parallel_count, heads_here * HEAD_SIZE)
     pair_replicas = jnp.repeat(
         key_value_pairs.reshape(local_row_count, KEY_VALUE_HEADS, 2 * HEAD_SIZE),
@@ -427,19 +586,6 @@
     context = lax.map(attend, jnp.arange(slice_length // block_rows, dtype=jnp.int32))
     block_width = heads_here * HEAD_SIZE
     context = context.reshape(slice_length, block_width)
-    experts = grp_count * sequence_parallel_count // HALVES
-    most_rows = max(2, local_row_count * TOP // experts)
-    if (grp_count, sequence_parallel_count) == (4, 8):
-        after_attention, expert_hidden, highest = back(
-            context,
-            residual,
-            norm_gain,
-            amax_history,
-            pick_rows(expert_ids, most_rows),
-            out_weight,
-            gate_up_weight[0],
-        )
-        return after_attention, expert_hidden[None], highest[0, :1]
     projected = lax.psum_scatter(
         jnp.dot(context, out_weight, preferred_element_type=jnp.float32).astype(jnp.bfloat16),
         "sp",

time: 259 us -> 173 us (0.67)
  blocking collectives: 69 us -> 0 us
  Pallas kernels: 146 us -> 163 us
  starting transfers between devices: 14.2 us -> 0 us
  waiting for transfers between devices: 11.4 us -> 0 us
  local copies, waits for them, and re-layouts: 11.6 us -> 6.6 us
    all_gather x1 -> x0, blocking collectives: 69 us -> none  [pick_rows(): everyone = lax.all_gather(expert_ids, ('grp', 'sp'), axis=0)]
    pallas_call x1, Pallas kernels: 146 us -> 163 us  [whole_layer(): pl.pallas_call(layer_kernel, out_shape=(jax.ShapeDtypeStruct((tokens, mod...]
    all_to_all x3 -> x0, starting transfers between devices: 14.2 us -> none  [the longest x1 7.25 us: per_device(): lax.all_to_all(doc_copies, 'sp', split_axis=1, concat_axis=0, tiled=True)]
    all_to_all x3 -> x0, waiting for transfers between devices: 11.4 us -> none  [the longest x1 6.92 us: per_device(): lax.all_to_all(pair_replicas, 'sp', split_axis=1, concat_axis=0, tiled=True)]
    reshape x3 -> x0, local copies, waits for them, and re-layouts: 2.92 us -> none  [the longest x1 1.88 us: per_device(): queries.reshape(local_row_count, sequence_parallel_count, heads_here * HE...]
  transfers between devices with their start and end apart: 3 -> 0, of which waited for: 2 -> 0; matrix products, arithmetic and copies ran while one was open for 2% -> 0% of each run, Pallas kernels for 0% -> 0%
where the time goes in v2:
time: 173 us; the launch traced here: 172 us
  Pallas kernels  163 us (94%)
  local copies, waits for them, and re-layouts  6.6 us (4%)
    pallas_call x1, Pallas kernels, whole_layer(): pl.pallas_call(layer_kernel, out_shape=(jax.ShapeDtypeStruct((tokens, mod...  163 us
    unnamed x3, local copies, waits for them, and re-layouts  4.73 us

profile of v2, /device:TPU:0, one launch (start us, length us, event | category | flops | bytes accessed | tf_op | source)
XLA Modules:
  0.0 172.3 jit_solution(3255921512690347291)
XLA Ops:
  0.6 0.7 convert_bitcast_fusion
  1.3 0.7 broadcast_in_dim.8.documents_ref
  2.0 0.8 copy.13
  2.7 0.2 fusion.1
  2.9 0.7 fusion.ranks_ref
  3.7 163.5 %attend_project_norm_dispatch.1 = (bf16[64,4096]{1,0:T(8,128)(2,1)}, bf16[1024,384]{1,0:T(8,128)(2,1)}, f32[8,128]{1,0:T(8,128)}) custom-call(bf16[64,4096]{1,0:T(8,128)(2,1)} %queries_ref.1, bf16[64,1024]{1,0:T(8,128)(2,1)} %pairs_ref.1, bf16[64,128]{1,0:T(8,128)(2,1)} %broadcast_in_dim.8.documents_ref, bf16[64,4096]{1,0:T(8,128)(2,1)} %residual_ref.1, ...), custom_call_target="tpu_custom_call" | custom-call | flops 12884901888 | bytes 12582912 | tf_op jit(solution)/shard_map/attend_project_norm_dispatch/pallas_call | solution.py:447
  167.1 1.2 slice.3
  168.3 1.9 %copy.16 = bf16[64,4096]{1,0:T(8,128)(2,1)} copy(bf16[64,4096]{1,0:T(8,128)(2,1)} %get-tuple-element.12) | data formatting | bytes 1048576
  170.2 2.1 %copy.17 = bf16[1,1024,384]{2,1,0:T(8,128)(2,1)} copy(bf16[1,1024,384]{2,1,0:T(8,128)(2,1)} %bitcast.7) | data formatting | bytes 1572864
  (1 shorter events, 0.0 us)

commit v3 on v2

--- a/solution.py
+++ b/solution.py
@@ -38,7 +38,7 @@
     residual_ref,
     gain_ref,
     history_ref,
-    ranks_ref,
+    expert_ids_ref,
     out_weight_ref,
     expert_weight_ref,
     after_ref,
@@ -47,6 +47,7 @@
     query_rows,
     pair_rows,
     pair_blocks,
+    document_tiles,
     context,
     out_weight,
     expert_weight,
@@ -104,11 +105,17 @@
         weight_chunk(k).start()
     expert_copy.start()
 
+    diagonal = lax.broadcasted_iota(jnp.int32, (tokens, 128), 1) == lax.broadcasted_iota(
+        jnp.int32, (tokens, 128), 0
+    )
+    own_documents = jnp.broadcast_to(documents_ref[...].astype(jnp.float32), (16, tokens))
+    document_tiles[sp] = jnp.dot(
+        own_documents.astype(jnp.bfloat16),
+        diagonal.astype(jnp.bfloat16),
+        preferred_element_type=jnp.float32,
+    ).astype(jnp.bfloat16)
     for head in range(KEY_VALUE_HEADS):
-        pair_blocks[head, :, : 2 * HEAD_SIZE] = pairs_ref[
-            :, head * 2 * HEAD_SIZE : (head + 1) * 2 * HEAD_SIZE
-        ]
-        pair_blocks[head, :, 2 * HEAD_SIZE :] = documents_ref[...]
+        pair_blocks[head] = pairs_ref[:, head * 2 * HEAD_SIZE : (head + 1) * 2 * HEAD_SIZE]
 
     barrier = pltpu.get_barrier_semaphore()
     partners = [sibling, x_peer, y_peer]
@@ -130,37 +137,81 @@
             :, pl.ds(pl.multiple_of(member * heads_width, heads_width), heads_width)
         ]
 
-    def head_copies(step, origin):
+    def query_copy(step, origin):
         target = lax.rem(sp + step, 8)
-        return (
-            copy_to(
-                pair_blocks.at[target // 2],
-                pair_rows.at[token_rows(origin)],
-                head_send_sems.at[0, step - 1],
-                head_receive_sems.at[0, step - 1],
-                (grp, target),
-            ),
-            copy_to(
-                query_columns(target),
-                query_rows.at[token_rows(origin)],
-                head_send_sems.at[1, step - 1],
-                head_receive_sems.at[1, step - 1],
-                (grp, target),
-            ),
+        return copy_to(
+            query_columns(target),
+            query_rows.at[token_rows(origin)],
+            head_send_sems.at[1, step - 1],
+            head_receive_sems.at[1, step - 1],
+            (grp, target),
+        )
+
+    def document_copy(step, origin):
+        return copy_to(
+            document_tiles.at[sp],
+            document_tiles.at[origin],
+            head_send_sems.at[2, step - 1],
+            head_receive_sems.at[2, step - 1],
+            (grp, lax.rem(sp + step, 8)),
+        )
+
+    def pair_line_copy(step, origin):
+        target = z_peer(step)
+        return copy_to(
+            pair_blocks.at[target],
+            pair_rows.at[token_rows(origin)],
+            head_send_sems.at[0, step - 1],
+            head_receive_sems.at[0, step - 1],
+            device(x, y, core, target),
+        )
+
+    def pair_across_copy(step, origin_x):
+        there = token_rows(2 * z_peer(4 - step) + origin_x)
+        return copy_to(
+            pair_rows.at[there],
+            pair_rows.at[there],
+            head_send_sems.at[0, 3 + step],
+            head_receive_sems.at[0, 3 + step],
+            x_peer,
         )
 
     for step in range(1, 8):
-        for copy in head_copies(step, sp):
-            copy.start()
+        document_copy(step, sp).start()
+    for step in (2, 1, 3):
+        pair_line_copy(step, sp).start()
+    for step in (4, 3, 5, 2, 6, 1, 7):
+        query_copy(step, sp).start()
     own_queries = pltpu.make_async_copy(
         query_columns(sp), query_rows.at[token_rows(sp)], local_sem.at[chunks + 1]
     )
     own_queries.start()
-    pair_rows[token_rows(sp)] = pair_blocks[sp // 2]
+    pair_rows[token_rows(sp)] = pair_blocks[z]
+    pair_across_copy(0, x).start()
+    for step in (1, 3, 2):
+        pair_line_copy(step, 2 * z_peer(4 - step) + x).wait_recv()
+        pair_across_copy(step, x).start()
     own_queries.wait()
     for step in range(1, 8):
-        for copy in head_copies(step, lax.rem(sp + 8 - step, 8)):
-            copy.wait_recv()
+        document_copy(step, lax.rem(sp + 8 - step, 8)).wait_recv()
+    for step in range(4):
+        pair_across_copy(step, 1 - x).wait_recv()
+    for step in range(1, 8):
+        query_copy(step, lax.rem(sp + 8 - step, 8)).wait_recv()
+
+    column_documents = jnp.zeros((16, 8 * tokens), jnp.float32)
+    for member in range(8):
+        place = (member % 2) * 4 + member // 2
+        shifted = lax.broadcasted_iota(jnp.int32, (128, 8 * tokens), 1) == (
+            lax.broadcasted_iota(jnp.int32, (128, 8 * tokens), 0) + place * tokens
+        )
+        inside = lax.broadcasted_iota(jnp.int32, (128, 8 * tokens), 0) < tokens
+        column_documents = column_documents + jnp.dot(
+            document_tiles[member],
+            (shifted & inside).astype(jnp.bfloat16),
+            preferred_element_type=jnp.float32,
+        )
+    column_documents = column_documents[:1]
 
     def attend(half):
         count = 4 * tokens
@@ -173,15 +224,10 @@
         column_position = (lax.div(column_place, tokens) * 2 + column_half) * tokens + lax.rem(
             column_place, tokens
         )
-        lanes = slice(2 * HEAD_SIZE, 3 * HEAD_SIZE)
-        first_lane = lax.broadcasted_iota(jnp.int32, (16, HEAD_SIZE), 1) == 0
-        column_documents = lax.dot_general(
-            first_lane.astype(jnp.bfloat16),
-            pair_rows[:, lanes],
-            (((1,), (1,)), ((), ())),
-            preferred_element_type=jnp.float32,
-        )[:1]
-        row_documents = pair_rows[here, lanes].astype(jnp.float32)[:, :1]
+        same_token = column == row + half * count
+        row_documents = jnp.sum(
+            jnp.where(same_token, column_documents, 0.0), axis=1, keepdims=True
+        )
         allowed = (column_position <= row_position) & (row_documents == column_documents)
 
         def one_head(head, carry):
@@ -264,7 +310,18 @@
 
     highest = lax.fori_loop(0, chunks, normalize, jnp.zeros((tokens, 1), jnp.float32))
 
-    rows[own_rows, pl.ds(model, 128)] = ranks_ref[...]
+    earlier = lax.broadcasted_iota(jnp.int32, (tokens, tokens), 1) < lax.broadcasted_iota(
+        jnp.int32, (tokens, tokens), 0
+    )
+    numbers = lax.broadcasted_iota(jnp.int32, (tokens, 128), 1)
+    named = jnp.zeros((tokens, 128), jnp.float32)
+    for choice in range(expert_ids_ref.shape[1]):
+        chosen = expert_ids_ref[:, choice : choice + 1] == numbers
+        named = jnp.maximum(named, jnp.where(chosen, 1.0, 0.0))
+    rank = jnp.dot(
+        earlier.astype(jnp.bfloat16), named.astype(jnp.bfloat16), preferred_element_type=jnp.float32
+    )
+    rows[own_rows, pl.ds(model, 128)] = jnp.where(named > 0.5, rank, -1.0).astype(jnp.bfloat16)
 
     started = []
 
@@ -371,11 +428,10 @@
         for line in range(4):
             arrived(slot(x, y, 1 - core, line))
 
-    lax.fori_loop(0, 1, compute, 0)
-    sibling_group(x, y)
-    lax.fori_loop(1, 2, compute, 0)
-
-    for line in nearest:
+    for number, line in enumerate(nearest):
+        if number == 3:
+            sibling_group(x, y)
+            lax.fori_loop(0, 2, compute, 0)
         place = slot(1 - x, y, core, line)
         arrived(place)
         pass_on(place, y_peer, 0, 0)
@@ -409,8 +465,12 @@
         else:
             pl.when(allowed)(lambda describe=describe: describe().wait_send())
     for step in range(1, 8):
-        for copy in head_copies(step, sp):
-            copy.wait_send()
+        query_copy(step, sp).wait_send()
+        document_copy(step, sp).wait_send()
+    for step in range(1, 4):
+        pair_line_copy(step, sp).wait_send()
+    for step in range(4):
+        pair_across_copy(step, x).wait_send()
 
     def drain(k, carry):
         pair_copy(k).wait_send()
@@ -428,7 +488,7 @@
     residual,
     norm_gain,
     amax_history,
-    ranks,
+    expert_ids,
     out_weight,
     expert_weight,
     devices,
@@ -443,7 +503,6 @@
     smem = pl.BlockSpec(memory_space=pltpu.SMEM)
     hbm = pl.BlockSpec(memory_space=pl.ANY)
     dma = pltpu.SemaphoreType.DMA
-    documents = jnp.broadcast_to(doc_ids.reshape(tokens, 1).astype(jnp.bfloat16), (tokens, 128))
     return pl.pallas_call(
         layer_kernel,
         out_shape=(
@@ -455,8 +514,9 @@
         out_specs=(vmem, vmem, vmem),
         scratch_shapes=[
             pltpu.VMEM((8 * tokens, block_width), jnp.bfloat16),
-            pltpu.VMEM((8 * tokens, 3 * HEAD_SIZE), jnp.bfloat16),
-            pltpu.VMEM((KEY_VALUE_HEADS, tokens, 3 * HEAD_SIZE), jnp.bfloat16),
+            pltpu.VMEM((8 * tokens, 2 * HEAD_SIZE), jnp.bfloat16),
+            pltpu.VMEM((KEY_VALUE_HEADS, tokens, 2 * HEAD_SIZE), jnp.bfloat16),
+            pltpu.VMEM((8, 16, 128), jnp.bfloat16),
             pltpu.VMEM((2, 4 * tokens, block_width), jnp.bfloat16),
             pltpu.VMEM((chunks, block_width, chunk), jnp.bfloat16),
             pltpu.VMEM(expert_weight.shape, jnp.bfloat16),
@@ -470,12 +530,12 @@
             dma((2, chunks)),
             dma((chunks, 3)),
             dma((chunks, 3)),
-            dma((40,)),
-            dma((devices, 2)),
+            dma((80,)),
+            dma((devices, 3)),
             dma((7,)),
             dma((7,)),
-            dma((2, 7)),
-            dma((2, 7)),
+            dma((3, 7)),
+            dma((3, 7)),
         ],
         compiler_params=pltpu.CompilerParams(
             collective_id=0, has_side_effects=True, vmem_limit_bytes=56 * 1024 * 1024
@@ -489,24 +549,14 @@
     )(
         queries,
         key_value_pairs,
-        documents,
+        doc_ids,
         residual,
         norm_gain.reshape(1, model),
         amax_history,
-        ranks,
+        expert_ids,
         out_weight,
         expert_weight,
     )
-
-
-def rank_table(expert_ids, experts):
-    local_row_count = expert_ids.shape[0]
-    numbers = jnp.arange(128, dtype=jnp.int32)
-    named = jnp.any(expert_ids[:, :, None] == numbers[None, None, :], axis=1)
-    order = jnp.arange(local_row_count, dtype=jnp.int32)
-    earlier = (order[None, :] < order[:, None]).astype(jnp.bfloat16)
-    rank = jnp.dot(earlier, named.astype(jnp.bfloat16), preferred_element_type=jnp.float32)
-    return jnp.where(named & (numbers < experts), rank, -1.0).astype(jnp.bfloat16)
 
 
 def per_device(
@@ -534,7 +584,7 @@
             residual,
             norm_gain,
             amax_history,
-            rank_table(expert_ids, experts),
+            expert_ids,
             out_weight,
             gate_up_weight[0],
             grp_count * sequence_parallel_count,

time: 173 us -> 168 us (0.971)
  Pallas kernels: 163 us -> 161 us
    pallas_call x1, Pallas kernels: 163 us -> 161 us  [whole_layer(): pl.pallas_call(layer_kernel, out_shape=(jax.ShapeDtypeStruct((tokens, mod...]
where the time goes in v3:
time: 168 us
  Pallas kernels  161 us (96%)
  local copies, waits for them, and re-layouts  6.53 us (4%)
    pallas_call x1, Pallas kernels, whole_layer(): pl.pallas_call(layer_kernel, out_shape=(jax.ShapeDtypeStruct((tokens, mod...  161 us
    unnamed x3, local copies, waits for them, and re-layouts  5.34 us

profile of v3, /device:TPU:0, one launch (start us, length us, event | category | flops | bytes accessed | tf_op | source)
XLA Modules:
  0.0 168.2 jit_solution(12866787685920446440)
XLA Ops:
  0.6 1.4 copy.12.expert_ids_ref
  2.0 161.0 %attend_project_norm_dispatch.1 = (bf16[64,4096]{1,0:T(8,128)(2,1)}, bf16[1024,384]{1,0:T(8,128)(2,1)}, f32[8,128]{1,0:T(8,128)}) custom-call(bf16[64,4096]{1,0:T(8,128)(2,1)} %queries_ref.1, bf16[64,1024]{1,0:T(8,128)(2,1)} %pairs_ref.1, s32[1,64]{1,0:T(1,128)} %documents_ref.1, bf16[64,4096]{1,0:T(8,128)(2,1)} %residual_ref.1, f32[1,4096]{1,0:T(1,128)} %bitcast.6, ...), custom_call_target="tpu_custom_call" | custom-call | flops 12884901888 | bytes 12582912 | tf_op jit(solution)/shard_map/attend_project_norm_dispatch/pallas_call | solution.py:506
  163.0 1.2 slice.3
  164.2 1.9 %copy.15 = bf16[64,4096]{1,0:T(8,128)(2,1)} copy(bf16[64,4096]{1,0:T(8,128)(2,1)} %get-tuple-element.12) | data formatting | bytes 1048576
  166.1 2.1 %copy.16 = bf16[1,1024,384]{2,1,0:T(8,128)(2,1)} copy(bf16[1,1024,384]{2,1,0:T(8,128)(2,1)} %bitcast.4) | data formatting | bytes 1572864
